TPU v7x, 32 devices: a whole 2x2x4 slice. The times are simulated.
32 devices in a mesh: groups: 2 (over y), replica: 4 (over z), tensor: 4 (over x, core).
Axes of the slice: x: 2, y: 2, z: 4, core: 2. Of those that a mesh axis runs over, the one named last changes fastest.
Arguments:
- features: bfloat16 [512, 8192], P(('groups', 'replica'), 'tensor'), parts along dimension 0, may hold values from -6 to 6
- base_query: bfloat16 [512, 8192], P(('groups', 'replica'), 'tensor'), parts along dimension 0, may hold values from -128 to 128
- base_key_value: bfloat16 [512, 2, 1024], P(('groups', 'replica'), None, 'tensor'), parts along dimension 0, may hold values from -6 to 6
- cached_key_rows: bfloat16 [512, 64, 1024], P(('groups', 'replica'), None, 'tensor'), parts along dimension 0, may hold values from -5 to 5
- cached_value_rows: bfloat16 [512, 64, 1024], P(('groups', 'replica'), None, 'tensor'), parts along dimension 0, may hold values from -6 to 6
- cache_length: int32 [512], P(('groups', 'replica')), parts along dimension 0, may hold values from 2 to 64, as said below
- row_adapter_index: int32 [512], P(('groups', 'replica')), parts along dimension 0, may hold values from 0 to 63, as said below
- adapter_storage_slot: int32 [128], P('groups'), parts along dimension 0, may hold values from 0 to 63, as said below
- adapter_down_maps: bfloat16 [64, 48, 8192], P('replica', None, 'tensor'), may hold values from -0.0625 to 0.0625
- query_up_maps: bfloat16 [64, 16, 8192], P('replica', None, 'tensor'), may hold values from -0.75 to 0.75
- key_value_up_maps: bfloat16 [64, 16, 2, 1024], P('replica', None, None, 'tensor'), may hold values from -0.75 to 0.75
- output_down_maps: bfloat16 [64, 16, 8192], P('replica', None, 'tensor'), may hold values from -0.0625 to 0.0625
- output_up_maps: bfloat16 [64, 16, 8192], P('replica', None, 'tensor'), may hold values from -1.5 to 1.5
Outputs:
- context: bfloat16 [512, 8192], P(('groups', 'replica'), 'tensor'), parts along dimension 0
- output_adjustment: bfloat16 [512, 8192], P(('groups', 'replica'), 'tensor'), parts along dimension 0
There are 2 independent parts, one for each index of `groups`. A program takes and returns all parts, laid end to end along the dimension named above; an argument that names none is the same for every part. Nothing has to cross between parts.
Inputs may be any that keep to these rules, and one draw needn't show every extreme that they name: `row_adapter_index`: adapter a is stored on replica adapter_storage_slot[a] // 16. In each aligned block of 64 rows (the rows of one replica) at most 32 rows use adapters stored on any one replica, and the adapters of one replica receive exactly 32 rows from every block. Each storage position once: adapter a is at position adapter_storage_slot[a] % 16 of the store of replica adapter_storage_slot[a] // 16. `cache_length`: some row of every aligned block of 64 rows attends to all 64 positions.
All inputs are finite; a program needn't handle non-finite values.
Results may differ from a plain program's by a relative error of at most 0.012.
Values may be sent and summed in bfloat16 or wider, within the bound.
A program may use at most 64 MiB of HBM per device.

v0:
```python
import math

import jax
import jax.numpy as jnp
from jax import lax
from jax.sharding import PartitionSpec as P

HEAD_DIM = 128


adapter_scale = 2.0
masked_score = -1e30


def reduce_coeffs(partial_value):
    return lax.psum(partial_value, "tensor").astype(jnp.bfloat16)


def send_back(result):
    return lax.all_to_all(result, "replica", split_axis=0, concat_axis=0, tiled=True)


def pick_coeffs(scratch_buffer, adapter_selector, down_flat, self_count):
    all_terms = lax.dot_general(
        scratch_buffer, down_flat, (((1,), (1,)), ((), ())), preferred_element_type=jnp.float32
    )
    all_terms = all_terms.reshape(scratch_buffer.shape[0], self_count, -1)
    partial_value = jnp.sum(adapter_selector.astype(jnp.float32)[:, :, None] * all_terms, axis=1)
    return reduce_coeffs(partial_value)


def expand(adapter_coefficients, adapter_selector):
    return (adapter_selector[:, :, None] * adapter_coefficients[:, None, :]).reshape(
        adapter_coefficients.shape[0], -1
    )


def projection_scratch(
    adapter_down_maps, query_up_maps, key_value_up_maps, scratch_buffer, adapter_selector
):
    self_count, coefficient_width, feature_width = adapter_down_maps.shape
    rank_span_width = coefficient_width // 3
    adapter_coefficients = pick_coeffs(
        scratch_buffer,
        adapter_selector,
        adapter_down_maps.reshape(self_count * coefficient_width, feature_width),
        self_count,
    )
    query_part = jnp.dot(
        expand(adapter_coefficients[:, :rank_span_width], adapter_selector),
        query_up_maps.reshape(self_count * rank_span_width, -1),
        preferred_element_type=jnp.float32,
    ).astype(jnp.bfloat16)
    key_part = jnp.dot(
        expand(adapter_coefficients[:, rank_span_width : 2 * rank_span_width], adapter_selector),
        key_value_up_maps[:, :, 0, :].reshape(self_count * rank_span_width, -1),
        preferred_element_type=jnp.float32,
    ).astype(jnp.bfloat16)
    value_part = jnp.dot(
        expand(adapter_coefficients[:, 2 * rank_span_width :], adapter_selector),
        key_value_up_maps[:, :, 1, :].reshape(self_count * rank_span_width, -1),
        preferred_element_type=jnp.float32,
    ).astype(jnp.bfloat16)
    return jnp.concatenate([query_part, key_part, value_part], axis=1)


def output_scratch(output_down_maps, output_up_maps, scratch_buffer, adapter_selector):
    self_count, rank_span_width, query_span_width = output_down_maps.shape
    adapter_coefficients = pick_coeffs(
        scratch_buffer,
        adapter_selector,
        output_down_maps.reshape(self_count * rank_span_width, query_span_width),
        self_count,
    )
    state_update = jnp.dot(
        expand(adapter_coefficients, adapter_selector),
        output_up_maps.reshape(self_count * rank_span_width, -1),
        preferred_element_type=jnp.float32,
    )
    return (adapter_scale * state_update).astype(jnp.bfloat16)


def attend(
    base_query,
    query_adjustment,
    cached_key_rows,
    cached_value_rows,
    newest_key,
    newest_value,
    cache_length,
):
    n_rows = base_query.shape[0]
    kv_local = cached_key_rows.shape[2] // HEAD_DIM
    group_size = base_query.shape[1] // HEAD_DIM // kv_local
    positions = cached_key_rows.shape[1]
    inverse_root = 1.0 / math.sqrt(HEAD_DIM)
    query_plain = base_query.reshape(n_rows, kv_local, group_size, HEAD_DIM)
    query_correction = query_adjustment.reshape(n_rows, kv_local, group_size, HEAD_DIM)
    cache_key_rows = cached_key_rows.reshape(n_rows, positions, kv_local, HEAD_DIM)
    cache_values = cached_value_rows.reshape(n_rows, positions, kv_local, HEAD_DIM)
    current_key = newest_key.reshape(n_rows, kv_local, HEAD_DIM)
    fresh_value = newest_value.reshape(n_rows, kv_local, HEAD_DIM)
    cache_score_rows = (
        jnp.einsum(
            "rkgd,rpkd->rkgp", query_plain, cache_key_rows, preferred_element_type=jnp.float32
        )
        + adapter_scale
        * jnp.einsum(
            "rkgd,rpkd->rkgp", query_correction, cache_key_rows, preferred_element_type=jnp.float32
        )
    ) * inverse_root
    self_scores = (
        jnp.einsum("rkgd,rkd->rkg", query_plain, current_key, preferred_element_type=jnp.float32)
        + adapter_scale
        * jnp.einsum(
            "rkgd,rkd->rkg", query_correction, current_key, preferred_element_type=jnp.float32
        )
    ) * inverse_root
    is_valid = (jnp.arange(positions)[None, :] < cache_length[:, None])[:, None, None, :]
    cache_score_rows = jnp.where(is_valid, cache_score_rows, masked_score)
    row_peak = jnp.maximum(jnp.max(cache_score_rows, axis=3), self_scores)
    cache_exp = jnp.where(is_valid, jnp.exp(cache_score_rows - row_peak[..., None]), 0.0)
    own_exp = jnp.exp(self_scores - row_peak)
    row_total = jnp.sum(cache_exp, axis=3) + own_exp
    cache_weights = (cache_exp / row_total[..., None]).astype(jnp.bfloat16)
    own_weights = (own_exp / row_total).astype(jnp.bfloat16)
    context = jnp.einsum(
        "rkgp,rpkd->rkgd", cache_weights, cache_values, preferred_element_type=jnp.float32
    )
    context = (
        context
        + own_weights.astype(jnp.float32)[..., None]
        * fresh_value.astype(jnp.float32)[:, :, None, :]
    )
    return context.astype(jnp.bfloat16).reshape(n_rows, -1)


def local(
    features,
    base_query,
    base_key_value,
    cached_key_rows,
    cached_value_rows,
    cache_length,
    row_adapter_index,
    adapter_storage_slot,
    adapter_down_maps,
    query_up_maps,
    key_value_up_maps,
    output_down_maps,
    output_up_maps,
):
    n_rows = features.shape[0]
    self_count = adapter_down_maps.shape[0]
    replicas = lax.axis_size("replica")
    my_index = lax.axis_index("replica")
    capacity = min(n_rows // 2, 2 * n_rows // replicas)
    table_hits = (
        row_adapter_index[:, None]
        == jnp.arange(adapter_storage_slot.shape[0], dtype=jnp.int32)[None, :]
    )
    row_slots = jnp.sum(jnp.where(table_hits, adapter_storage_slot[None, :], 0), axis=1)
    owners = row_slots // self_count
    local_slot = row_slots % self_count
    owner_hits = (owners[:, None] == jnp.arange(replicas, dtype=jnp.int32)[None, :]).astype(
        jnp.int32
    )
    row_ranks = jnp.sum(jnp.cumsum(owner_hits, axis=0) * owner_hits, axis=1) - 1
    row_target = owners * capacity + row_ranks
    placing = (
        row_target[None, :] == jnp.arange(replicas * capacity, dtype=jnp.int32)[:, None]
    ).astype(jnp.bfloat16)

    def route(source, work):
        row_codes = jnp.stack([owners, local_slot], axis=1).astype(jnp.bfloat16)
        all_source, all_codes = (
            lax.all_gather(source, "replica", axis=0, tiled=True),
            lax.all_gather(row_codes, "replica", axis=0, tiled=True),
        )
        all_codes = all_codes.astype(jnp.int32)
        is_mine = all_codes[:, 0] == my_index
        block_rank = (
            jnp.cumsum(is_mine.reshape(replicas, n_rows).astype(jnp.int32), axis=1) - 1
        ).reshape(-1)
        anchor = jnp.arange(replicas * n_rows, dtype=jnp.int32) // n_rows
        target = jnp.where(is_mine, anchor * capacity + block_rank, -1)
        gathering = (
            target[None, :] == jnp.arange(replicas * capacity, dtype=jnp.int32)[:, None]
        ).astype(jnp.bfloat16)
        all_select = (all_codes[:, 1:2] == jnp.arange(self_count, dtype=jnp.int32)[None, :]).astype(
            jnp.bfloat16
        )
        scratch_buffer = jnp.dot(gathering, all_source, preferred_element_type=jnp.float32).astype(
            jnp.bfloat16
        )
        adapter_selector = jnp.dot(
            gathering, all_select, preferred_element_type=jnp.float32
        ).astype(jnp.bfloat16)
        replies = send_back(work(scratch_buffer, adapter_selector).reshape(replicas, capacity, -1))
        flat_replies = replies.reshape(replicas * capacity, -1)
        unpacked = lax.dot_general(
            placing, flat_replies, (((0,), (0,)), ((), ())), preferred_element_type=jnp.float32
        )
        return unpacked.astype(jnp.bfloat16)

    def first_work(scratch_buffer, adapter_selector):
        return projection_scratch(
            adapter_down_maps, query_up_maps, key_value_up_maps, scratch_buffer, adapter_selector
        )

    def second_work(scratch_buffer, adapter_selector):
        return output_scratch(output_down_maps, output_up_maps, scratch_buffer, adapter_selector)

    deltas = route(features, first_work)
    query_span_width = base_query.shape[1]
    key_width = base_key_value.shape[2]
    query_adjustment = deltas[:, :query_span_width]
    key_adjustment = deltas[:, query_span_width : query_span_width + key_width]
    value_adjustment = deltas[:, query_span_width + key_width :]
    newest_key = (
        base_key_value[:, 0, :].astype(jnp.float32)
        + adapter_scale * key_adjustment.astype(jnp.float32)
    ).astype(jnp.bfloat16)
    newest_value = (
        base_key_value[:, 1, :].astype(jnp.float32)
        + adapter_scale * value_adjustment.astype(jnp.float32)
    ).astype(jnp.bfloat16)
    context = attend(
        base_query,
        query_adjustment,
        cached_key_rows,
        cached_value_rows,
        newest_key,
        newest_value,
        cache_length,
    )
    output_adjustment = route(context, second_work)
    return (context, output_adjustment)


def solution(mesh):
    return jax.shard_map(
        local,
        mesh=mesh,
        in_specs=(
            P(("groups", "replica"), "tensor"),
            P(("groups", "replica"), "tensor"),
            P(("groups", "replica"), None, "tensor"),
            P(("groups", "replica"), None, "tensor"),
            P(("groups", "replica"), None, "tensor"),
            P(("groups", "replica")),
            P(("groups", "replica")),
            P("groups"),
            P("replica", None, "tensor"),
            P("replica", None, "tensor"),
            P("replica", None, None, "tensor"),
            P("replica", None, "tensor"),
            P("replica", None, "tensor"),
        ),
        out_specs=(P(("groups", "replica"), "tensor"), P(("groups", "replica"), "tensor")),
        check_vma=False,
    )
```

profile of v0, /device:TPU:0, one launch (start us, length us, event | category | flops | bytes accessed | tf_op | source)
XLA Modules:
  0.0 158.3 jit_solution(6433421211840617257)
XLA Ops:
  7.2 0.0 copy-start
  7.2 0.0 all-gather.4.cloned.1.call-start
  7.2 0.7 all-gather.4.cloned.1.call-update
  7.9 1.0 select_reduce_fusion.1
  9.0 12.6 %all-gather = bf16[4,64,2]{1,2,0:T(2,128)(2,1)S(1)} all-gather(bf16[1,64,2]{1,2,0:T(2,128)(2,1)S(1)} %maximum_bitcast_fusion), channel_id=1, replica_groups=mesh['groups'=2,'replica'=4,'tensor'=4] {'replica'}, dimensions={0}, use_global_device_ids=true | all-gather | bytes 1280 | tf_op jit(solution)/shard_map/all_gather | solution.py:178
  21.6 0.1 reshape.262
  21.7 0.1 reshape.256
  21.8 0.2 reduce_window_sum.24
  22.0 0.1 sub.42
  22.1 1.6 %fusion.69 = (bf16[16,16,1,256]{3,2,1,0:T(2,128)(2,1)S(1)}, bf16[16,16,1,256]{3,2,1,0:T(2,128)(2,1)S(1)}) fusion(bf16[16,16,2,256]{3,2,1,0:T(2,128)(2,1)} %param.23), kind=kLoop, calls=%fused_computation.108 | loop fusion | bytes 524288 | tf_op jit(solution)/shard_map/slice | solution.py:56
  23.8 0.0 copy-start.8
  23.8 0.3 fusion.72
  24.1 16.1 %all-gather.4.cloned.1.call-done = bf16[256,2048]{1,0:T(8,128)(2,1)} async-done(((bf16[64,2048]{1,0:T(8,128)(2,1)}), bf16[256,2048]{1,0:T(8,128)(2,1)}) %all-gather.4.cloned.1.call-update) | async-done | bytes 1048592 | tf_op jit(solution)/shard_map/all_gather | solution.py:177
  40.2 0.0 copy-done.8
  40.3 0.0 copy-done.6
  40.3 0.0 copy-done
  40.3 2.4 %fusion.32 = f32[128,48]{0,1:T(8,128)S(1)} fusion(bf16[16,48,2048]{2,1,0:T(8,128)(2,1)S(1)} %copy-done, bf16[256,2048]{1,0:T(8,128)(2,1)} %all-gather.4.cloned.1.call-done, f32[128,16]{0,1:T(8,128)S(1)} %get-tuple-element.19, s32[256]{0:T(256)S(1)} %fusion.63), kind=kOutput, calls=%fused_computation.27 | convolution fusion | flops 537356288 | bytes 4228096 | tf_op jit(solution)/shard_map/dot_general | solution.py:24
  42.7 10.9 %psum.14 = bf16[128,48]{0,1:T(8,128)(2,1)S(1)} all-reduce(f32[128,48]{0,1:T(8,128)S(1)} %fusion.32), channel_id=1, replica_groups=mesh['groups'=2,'replica'=4,'tensor'=4] {'tensor'}, use_global_device_ids=true, to_apply=%region_5.6 | all-reduce | flops 6144 | bytes 36864 | tf_op jit(solution)/shard_map/psum | solution.py:16
  53.6 0.2 convolution_convert_fusion.4
  53.8 0.2 convolution_convert_fusion.5
  54.0 0.0 copy-done.4
  54.0 0.0 copy-start.12
  54.0 0.0 copy-start.2
  54.0 1.6 %fusion.1 = bf16[128,2048]{1,0:T(8,128)(2,1)S(1)} fusion(bf16[16,16,2048]{2,1,0:T(8,128)(2,1)} %param.22, bf16[128,16]{0,1:T(8,128)(2,1)S(1)} %get-tuple-element.10, bf16[128,16]{0,1:T(8,128)(2,1)S(1)} %get-tuple-element.20), kind=kOutput, calls=%fused_computation.4 | convolution fusion | flops 134512640 | bytes 1581056 | tf_op jit(solution)/shard_map/dot_general | solution.py:49
  55.6 0.9 pad_maximum_fusion
  56.6 4.2 %all-to-all-start = ((bf16[4,32,2560]{2,1,0:T(8,128)(2,1)}), bf16[4,32,2560]{2,1,0:T(8,128)(2,1)}, u32[]{:S(2)}, u32[]{:S(2)}) async-start(bf16[4,32,2560]{2,1,0:T(8,128)(2,1)} %bitcast.149), calls=%async_computation | async-start | bytes 1310720 | tf_op jit(solution)/shard_map/all_to_all | solution.py:20
  60.7 0.0 all-gather.6.cloned.1.call-start
  60.8 0.1 fusion.56
  60.8 0.1 reduce_window_sum.23
  60.9 1.0 copy.79
  61.9 0.2 select_reduce_fusion
  62.1 0.0 copy-done.12
  62.1 0.0 copy-start.10
  62.1 0.1 iota_compare_fusion.13
  62.2 0.7 fusion.70
  63.0 14.9 %all-to-all-done = bf16[4,32,2560]{2,1,0:T(8,128)(2,1)} async-done(((bf16[4,32,2560]{2,1,0:T(8,128)(2,1)}), bf16[4,32,2560]{2,1,0:T(8,128)(2,1)}, u32[]{:S(2)}, u32[]{:S(2)}) %all-to-all-start) | async-done | bytes 655392 | tf_op jit(solution)/shard_map/all_to_all | solution.py:20
  77.9 1.4 convolution_convert_fusion
  79.3 0.7 copy.80
  80.1 0.9 fusion.40
  81.0 0.6 reshape.271
  81.6 1.9 %fusion.75 = f32[64,2,1,8]{3,2,1,0:T(1,128)} fusion(bf16[64,2,8,128]{3,2,1,0:T(8,128)(2,1)} %bitcast.156, bf16[64,2,128,1]{2,3,1,0:T(2,128)(2,1)} %reshape.271), kind=kOutput, calls=%fused_computation.114 | convolution fusion | flops 262144 | bytes 299008 | tf_op jit(solution)/shard_map/rkgd,rkd->rkg/dot_general | solution.py:115
  83.5 0.9 copy.72
  84.4 3.0 %fusion.23 = f32[64,2,8,64]{3,2,1,0:T(8,128)S(1)} fusion(bf16[64,2,8,128]{3,2,1,0:T(8,128)(2,1)} %bitcast.157, bf16[64,64,256]{2,1,0:T(8,128)(2,1)} %param.16), kind=kOutput, calls=%fused_computation.23 | convolution fusion | flops 16842752 | bytes 2621440 | tf_op jit(solution)/shard_map/rkgd,rpkd->rkgp/dot_general | solution.py:108
  87.4 0.0 copy-done.3
  87.4 0.9 fusion.74
  88.3 2.0 %fusion.73 = (f32[64,2,8]{2,1,0:T(2,128)S(1)}, f32[64,2,8,64]{3,2,1,0:T(8,128)}) fusion(f32[64,2,8,64]{3,2,1,0:T(8,128)S(1)} %fusion.23, bf16[64,2,8,128]{3,2,1,0:T(8,128)(2,1)S(1)} %bitcast.155, pred[64,64]{1,0:T(8,128)(4,1)S(1)} %iota_compare_fusion.13, bf16[64,64,256]{2,1,0:T(8,128)(2,1)S(1)} %copy-done.1), kind=kOutput, calls=%fused_computation.112 | convolution fusion | flops 17038336 | bytes 2891776 | tf_op jit(solution)/shard_map/rkgd,rpkd->rkgp/dot_general | solution.py:104
  90.4 0.1 copy.63
  90.4 0.9 copy.71
  91.4 0.1 copy.64
  91.5 1.4 fusion.34
  92.9 0.1 copy.65
  93.0 0.1 copy.66
  93.1 0.1 copy.68
  93.3 2.5 %fusion.29 = bf16[64,2,8,128]{3,2,1,0:T(8,128)(2,1)S(1)} fusion(f32[64,2,8,64]{3,2,1,0:T(8,128)} %get-tuple-element.22, f32[64,2,128]{2,1,0:T(2,128)S(1)} %reshape.259, f32[64,2,8]{2,1,0:T(2,128)S(1)} %copy.68, f32[64,2,8]{2,1,0:T(2,128)S(1)} %copy.66, f32[64,2,8]{2,1,0:T(2,128)S(1)} %copy.64, pred[64,64]{1,0:T(8,128)(4,1)S(1)} %iota_compare_fusion.13, ...), kind=kOutput, calls=%fused_computation.25 | convolution fusion | flops 17432576 | bytes 2703360 | tf_op jit(solution)/shard_map/rkgp,rpkd->rkgd/dot_general | solution.py:127
  95.8 0.8 copy.116
  96.6 0.0 all-gather.6.cloned.1.call-update
  96.6 0.0 copy-start.11
  96.6 26.8 %all-gather.6.cloned.1.call-done = bf16[256,2048]{1,0:T(8,128)(2,1)} async-done(((bf16[64,2048]{1,0:T(8,128)(2,1)}), bf16[256,2048]{1,0:T(8,128)(2,1)}) %all-gather.6.cloned.1.call-update) | async-done | bytes 1048592 | tf_op jit(solution)/shard_map/all_gather | solution.py:177
  123.4 0.0 copy-done.9
  123.4 2.2 %fusion.33 = f32[128,16]{0,1:T(8,128)S(1)} fusion(bf16[16,16,2048]{2,1,0:T(8,128)(2,1)} %param.24, bf16[256,2048]{1,0:T(8,128)(2,1)} %all-gather.6.cloned.1.call-done, f32[128,16]{0,1:T(8,128)S(1)} %copy-done.7, s32[256]{0:T(256)S(1)} %copy-done.9), kind=kOutput, calls=%fused_computation.31 | convolution fusion | flops 268793856 | bytes 2114560 | tf_op jit(solution)/shard_map/dot_general | solution.py:24
  125.6 6.5 %psum.15 = bf16[128,16]{0,1:T(8,128)(2,1)S(1)} all-reduce(f32[128,16]{0,1:T(8,128)S(1)} %fusion.33), channel_id=1, replica_groups=mesh['groups'=2,'replica'=4,'tensor'=4] {'tensor'}, use_global_device_ids=true, to_apply=%region_9.10 | all-reduce | flops 2048 | bytes 12288 | tf_op jit(solution)/shard_map/psum | solution.py:16
  132.2 1.6 fusion.2
  133.7 16.8 %all_to_all.10 = bf16[4,32,2048]{2,1,0:T(8,128)(2,1)S(1)} all-to-all(bf16[4,32,2048]{2,1,0:T(8,128)(2,1)S(1)} %bitcast.150), channel_id=1, replica_groups=mesh['groups'=2,'replica'=4,'tensor'=4] {'replica'}, dimensions={0} | all-to-all | bytes 1048576 | tf_op jit(solution)/shard_map/all_to_all | solution.py:20
  150.5 1.0 convolution_convert_fusion.3
  (30 shorter events, 0.3 us)
Async XLA Ops:
  7.2 33.1 %copy-start = (bf16[16,48,2048]{2,1,0:T(8,128)(2,1)S(1)}, bf16[16,48,2048]{2,1,0:T(8,128)(2,1)}, u32[]{:S(2)}) copy-start(bf16[16,48,2048]{2,1,0:T(8,128)(2,1)} %param.21) | copy-start | bytes 9437188
  7.2 33.1 %all-gather.4.cloned.1.call-start = ((), (), s32[]{:S(2)}) async-start(), calls=%async_computation.2 | async-start | bytes 1310720 | tf_op jit(solution)/shard_map/all_gather | solution.py:177
  23.8 16.4 %copy-start.8 = (s32[256]{0:T(256)}, s32[256]{0:T(256)S(1)}, u32[]{:S(2)}) copy-start(s32[256]{0:T(256)S(1)} %fusion.63) | copy-start | bytes 3076
  24.1 16.2 %copy-start.6 = (f32[128,16]{0,1:T(8,128)}, f32[128,16]{0,1:T(8,128)S(1)}, u32[]{:S(2)}) copy-start(f32[128,16]{0,1:T(8,128)S(1)} %get-tuple-element.19) | copy-start | bytes 24580
  24.1 29.9 %copy-start.4 = (bf16[128,16]{0,1:T(8,128)(2,1)}, bf16[128,16]{0,1:T(8,128)(2,1)S(1)}, u32[]{:S(2)}) copy-start(bf16[128,16]{0,1:T(8,128)(2,1)S(1)} %get-tuple-element.20) | copy-start | bytes 12292
  54.0 8.1 %copy-start.12 = (s32[64]{0:T(128)S(1)}, s32[64]{0:T(128)}, u32[]{:S(2)}) copy-start(s32[64]{0:T(128)} %param.18) | copy-start | bytes 772
  54.0 8.2 %copy-start.2 = (bf16[64,2,256]{2,1,0:T(2,128)(2,1)S(1)}, bf16[64,2,256]{2,1,0:T(2,128)(2,1)}, u32[]{:S(2)}) copy-start(bf16[64,2,256]{2,1,0:T(2,128)(2,1)} %param.15) | copy-start | bytes 196612
  56.6 21.4 %all-to-all-start = ((bf16[4,32,2560]{2,1,0:T(8,128)(2,1)}), bf16[4,32,2560]{2,1,0:T(8,128)(2,1)}, u32[]{:S(2)}, u32[]{:S(2)}) async-start(bf16[4,32,2560]{2,1,0:T(8,128)(2,1)} %bitcast.149), calls=%async_computation | async-start | bytes 1310720 | tf_op jit(solution)/shard_map/all_to_all | solution.py:20
  60.7 62.7 %all-gather.6.cloned.1.call-start = ((), (), s32[]{:S(2)}) async-start(), calls=%async_computation.3 | async-start | bytes 1310720 | tf_op jit(solution)/shard_map/all_gather | solution.py:177
  62.1 17.9 %copy-start.10 = (s32[64]{0:T(128)}, s32[64]{0:T(128)S(1)}, u32[]{:S(2)}) copy-start(s32[64]{0:T(128)S(1)} %add_add_fusion) | copy-start | bytes 772
  81.6 5.8 %copy-start.3 = (bf16[64,2,128,1]{2,3,1,0:T(2,128)(2,1)S(1)}, bf16[64,2,128,1]{2,3,1,0:T(2,128)(2,1)}, u32[]{:S(2)}) copy-start(bf16[64,2,128,1]{2,3,1,0:T(2,128)(2,1)} %reshape.271) | copy-start | bytes 98308
  84.4 3.9 %copy-start.1 = (bf16[64,64,256]{2,1,0:T(8,128)(2,1)S(1)}, bf16[64,64,256]{2,1,0:T(8,128)(2,1)}, u32[]{:S(2)}) copy-start(bf16[64,64,256]{2,1,0:T(8,128)(2,1)} %param.16) | copy-start | bytes 6291460
  93.3 30.1 %copy-start.7 = (f32[128,16]{0,1:T(8,128)S(1)}, f32[128,16]{0,1:T(8,128)}, u32[]{:S(2)}) copy-start(f32[128,16]{0,1:T(8,128)} %copy-done.6) | copy-start | bytes 24580
  93.3 30.1 %copy-start.9 = (s32[256]{0:T(256)S(1)}, s32[256]{0:T(256)}, u32[]{:S(2)}) copy-start(s32[256]{0:T(256)} %copy-done.8) | copy-start | bytes 3076
  95.8 36.4 %copy-start.5 = (bf16[128,16]{0,1:T(8,128)(2,1)S(1)}, bf16[128,16]{0,1:T(8,128)(2,1)}, u32[]{:S(2)}) copy-start(bf16[128,16]{0,1:T(8,128)(2,1)} %copy-done.4) | copy-start | bytes 12292
  96.6 53.9 %copy-start.11 = (s32[64]{0:T(128)S(1)}, s32[64]{0:T(128)}, u32[]{:S(2)}) copy-start(s32[64]{0:T(128)} %copy-done.10) | copy-start | bytes 772
Sparse Core Ops, SparseCore 0:
  9.6 30.6 all-gather.3
  96.7 26.6 all-gather.5
where the time goes:
time: 159 us; the launch traced here: 158 us
  waiting for transfers between devices  58.6 us (37%)
  blocking collectives  46.7 us (29%)
  matrix products  21.1 us (13%)
  between operations  14.3 us (9%)
  local copies, waits for them, and re-layouts  8.2 us (5%)
  other arithmetic  5.1 us (3%)
  starting transfers between devices  4.23 us (3%)
    all_gather x2, waiting for transfers between devices, route(): lax.all_gather(source, 'replica', axis=0, tiled=True)  42.9 us
    psum x2, blocking collectives, reduce_coeffs(): return lax.psum(partial_value, 'tensor').astype(jnp.bfloat16)  17.4 us
    all_to_all x1, blocking collectives, send_back(): lax.all_to_all(result, 'replica', split_axis=0, concat_axis=0, tiled=True)  16.8 us
    all_to_all x1, waiting for transfers between devices, send_back(): lax.all_to_all(result, 'replica', split_axis=0, concat_axis=0, tiled=True)  14.9 us
    all_gather x1, blocking collectives, route(): lax.all_gather(row_codes, 'replica', axis=0, tiled=True)  12.6 us
    dot_general x2, matrix products, pick_coeffs(): lax.dot_general(scratch_buffer, down_flat, (((1,), (1,)), ((), ())), pref...  4.62 us
    all_to_all x1, starting transfers between devices, send_back(): lax.all_to_all(result, 'replica', split_axis=0, concat_axis=0, tiled=True)  4.15 us
  transfers between devices with their start and end apart: 3, of which 3 were waited for; matrix products, arithmetic and copies ran while one was open for 4% of the time, Pallas kernels for 0%

commit v1 on v0

v1 whole, which is shorter than its diff:
```python
import functools
import math

import jax
import jax.numpy as jnp
from jax import lax
from jax.experimental import pallas as pl
from jax.experimental.pallas import tpu as pltpu
from jax.sharding import PartitionSpec as P

HEAD_DIM = 128
LANES = 128
BLOCK_ROWS = 4

adapter_scale = 2.0
masked_score = -1e30
BF16 = jnp.bfloat16
F32 = jnp.float32

NN = (((1,), (0,)), ((), ()))
NT = (((1,), (1,)), ((), ()))


def mm(a, b, dims=NN):
    return lax.dot_general(a, b, dims, preferred_element_type=F32)


def iota(shape, dim):
    return lax.broadcasted_iota(jnp.int32, shape, dim)


def one_hot(hit):
    return jnp.where(hit, 1.0, 0.0).astype(BF16)


def kernel(
    replicas,
    tensors,
    cap,
    rank,
    index_ref,
    table_ref,
    length_ref,
    feature_ref,
    query_ref,
    key_value_ref,
    key_hbm,
    value_hbm,
    down_hbm,
    query_up_hbm,
    key_value_up_hbm,
    out_down_hbm,
    out_up_hbm,
    context_ref,
    adjust_ref,
    keys,
    values,
    down,
    query_up,
    key_value_up,
    out_down,
    out_up,
    feature_send,
    feature_recv,
    coeff_recv,
    delta_send,
    delta_recv,
    context_send,
    context_recv,
    out_coeff_recv,
    adjust_send,
    adjust_recv,
    base_heads,
    delta_heads,
    context_heads,
    base_scores,
    load_sems,
    feature_sems,
    coeff_sems,
    delta_sems,
    context_sems,
    out_coeff_sems,
    adjust_sems,
):
    n_rows, width = feature_ref.shape
    query_width = query_ref.shape[1]
    kv_width = key_value_ref.shape[1] // 2
    groups = kv_width // HEAD_DIM
    heads = query_width // HEAD_DIM // groups
    group_width = heads * HEAD_DIM
    positions = key_hbm.shape[1]
    adapters = table_ref.shape[1]
    own = out_down_hbm.shape[0] // rank
    slots = replicas * cap
    inverse_root = 1.0 / math.sqrt(HEAD_DIM)
    me = lax.axis_index("replica")
    my_tensor = lax.axis_index("tensor")

    def ahead(k):
        return lax.rem(me + k, replicas)

    def behind(k):
        return lax.rem(me + replicas - k, replicas)

    loads = []
    for i, (source, target) in enumerate(
        (
            (key_hbm, keys),
            (down_hbm, down),
            (value_hbm, values),
            (query_up_hbm, query_up),
            (key_value_up_hbm, key_value_up),
            (out_down_hbm, out_down),
            (out_up_hbm, out_up),
        )
    ):
        load = pltpu.make_async_copy(source, target, load_sems.at[i])
        load.start()
        loads.append(load)
    (
        keys_load,
        down_load,
        values_load,
        query_up_load,
        key_value_up_load,
        out_down_load,
        out_up_load,
    ) = loads

    barrier = pltpu.get_barrier_semaphore()
    for k in range(1, replicas):
        pl.semaphore_signal(
            barrier,
            inc=1,
            device_id={"replica": ahead(k)},
            device_id_type=pl.DeviceIdType.MESH,
        )
    for t in range(1, tensors):
        pl.semaphore_signal(
            barrier,
            inc=1,
            device_id={"tensor": lax.rem(my_tensor + t, tensors)},
            device_id_type=pl.DeviceIdType.MESH,
        )

    def remote(source, target, sems, i, device):
        copy = pltpu.make_async_remote_copy(
            src_ref=source,
            dst_ref=target,
            send_sem=sems.at[0, i],
            recv_sem=sems.at[1, i],
            device_id=device,
            device_id_type=pl.DeviceIdType.MESH,
        )
        copy.start()
        return copy

    table = table_ref[...]
    table_owner = table // own
    table_local = table - table_owner * own
    pair = jnp.where(iota((8, adapters), 0) == 0, table_owner, table_local)
    adapter_hits = one_hot(iota((adapters, n_rows), 0) == index_ref[...])
    looked_up = mm(pair.astype(F32).astype(BF16), adapter_hits).astype(jnp.int32)
    owner = looked_up[0:1]
    local_slot = looked_up[1:2]
    relative = owner - me
    relative = jnp.where(relative < 0, relative + replicas, relative)
    replica_rows = max(8, replicas)
    owner_hits = iota((replica_rows, n_rows), 0) == relative
    before = one_hot(iota((n_rows, n_rows), 0) <= iota((n_rows, n_rows), 1))
    counts = mm(one_hot(owner_hits), before)
    row_rank = jnp.sum(jnp.where(owner_hits, counts, 0.0), axis=0, keepdims=True) - 1.0
    row_target = relative * cap + row_rank.astype(jnp.int32)
    placing = one_hot(iota((slots, n_rows), 0) == row_target)
    identity = one_hot(iota((n_rows, n_rows), 0) == iota((n_rows, n_rows), 1))
    unplacing = mm(identity, placing, NT).astype(BF16)
    slot_hits = one_hot(iota((LANES, n_rows), 0) == local_slot)
    selectors = mm(placing, slot_hits, NT).astype(BF16)

    packed = mm(placing, feature_ref[...]).astype(BF16)
    feature_recv[0, :, :width] = packed[:cap]
    feature_recv[0, :, width:] = selectors[:cap]
    for k in range(1, replicas):
        feature_send[k, :, :width] = packed[k * cap : (k + 1) * cap]
        feature_send[k, :, width:] = selectors[k * cap : (k + 1) * cap]
    pl.semaphore_wait(barrier, replicas + tensors - 2)
    feature_copies = [None] + [
        remote(
            feature_send.at[k], feature_recv.at[k], feature_sems, k, {"replica": ahead(k)}
        )
        for k in range(1, replicas)
    ]

    score_rows = n_rows * heads
    block_columns = BLOCK_ROWS * positions
    block_heads = BLOCK_ROWS * heads
    for g in range(groups):
        for h in range(heads):
            column = (g * heads + h) * HEAD_DIM
            base_heads[g, pl.ds(h, n_rows, stride=heads), :] = query_ref[
                :, column : column + HEAD_DIM
            ].astype(F32)
    blocks = n_rows // BLOCK_ROWS
    step_blocks = min(8, blocks)
    steps = blocks // step_blocks
    step_rows = step_blocks * BLOCK_ROWS
    step_heads = step_blocks * block_heads

    def block_of(ref, step, g):
        block = ref[
            pl.ds(pl.multiple_of(step * step_rows, step_rows), step_rows),
            :,
            g * HEAD_DIM : (g + 1) * HEAD_DIM,
        ]
        return block.reshape(step_blocks, block_columns, HEAD_DIM)

    def heads_of(step):
        return pl.ds(pl.multiple_of(step * step_heads, step_heads), step_heads)

    def score(query, key):
        return lax.dot_general(
            query.reshape(step_blocks, block_heads, HEAD_DIM),
            key,
            (((2,), (2,)), ((0,), (0,))),
            preferred_element_type=F32,
        ).reshape(step_heads, block_columns)

    def row_hits(step):
        head_row = iota((step_heads, n_rows), 0) // heads + step * step_rows
        return head_row == iota((step_heads, n_rows), 1)

    lengths = length_ref[...].astype(F32)
    keys_load.wait()

    def base_step(step, carry):
        spread = jnp.where(row_hits(step), lengths, 0.0).astype(BF16)
        head_lengths = mm(spread, jnp.ones((n_rows, block_columns), BF16))
        column = iota((step_heads, block_columns), 1)
        row = iota((step_heads, block_columns), 0)
        valid = ((row // heads) % BLOCK_ROWS == column // positions) & (
            (column % positions).astype(F32) < head_lengths
        )
        for g in range(groups):
            found = score(base_heads[g, heads_of(step), :].astype(BF16), block_of(keys, step, g))
            base_scores[g, heads_of(step), :] = jnp.where(
                valid, found * inverse_root, masked_score
            )
        return carry

    lax.fori_loop(0, steps, base_step, 0)

    bundles = [[k] for k in range(replicas)] if replicas <= 4 else [list(range(replicas))]
    down_load.wait()
    coeff_parts = []
    selector_parts = []
    chooser = one_hot(iota((own, LANES), 0) == iota((own, LANES), 1))

    def fold(terms, selector):
        stacked = terms.reshape(own, terms.shape[0] // own, terms.shape[1])
        return jnp.sum(stacked * selector[:, None, :], axis=0)

    for bundle in bundles:
        for k in bundle:
            if k:
                feature_copies[k].wait()
        received = feature_recv[bundle[0] : bundle[-1] + 1].reshape(len(bundle) * cap, -1)
        selector = mm(chooser, received[:, width:], NT)
        selector_parts.append(selector)
        coeff_parts.append(fold(mm(down[...], received[:, :width], NT), selector))
    selector = jnp.concatenate(selector_parts, axis=1)

    def sum_over_tensor(parts, recv, sems):
        for bundle, part in zip(bundles, parts):
            recv[0, :, bundle[0] * cap : (bundle[-1] + 1) * cap] = part
        copies = [
            remote(
                recv.at[0],
                recv.at[t],
                sems,
                t,
                {"tensor": lax.rem(my_tensor + t, tensors)},
            )
            for t in range(1, tensors)
        ]
        for copy in copies:
            copy.wait()
        total = recv[0]
        for t in range(1, tensors):
            total = total + recv[t]
        return total.astype(BF16).astype(F32)

    def expand(coeffs):
        spread = selector[:, None, :] * coeffs[None, :, :]
        return spread.reshape(own * rank, slots).T.astype(BF16)

    coeffs = sum_over_tensor(coeff_parts, coeff_recv, coeff_sems)
    query_coeffs = expand(coeffs[:rank])
    key_coeffs = expand(coeffs[rank : 2 * rank])
    value_coeffs = expand(coeffs[2 * rank :])

    query_up_load.wait()
    key_value_up_load.wait()
    delta_copies = []
    for g in range(groups):
        sent = [
            mm(query_coeffs, query_up[:, g * group_width : (g + 1) * group_width]),
            mm(key_coeffs, key_value_up[:, g * HEAD_DIM : (g + 1) * HEAD_DIM]),
            mm(
                value_coeffs,
                key_value_up[:, kv_width + g * HEAD_DIM : kv_width + (g + 1) * HEAD_DIM],
            ),
        ]
        sent = jnp.concatenate([x.astype(BF16) for x in sent], axis=1)
        delta_recv[g, 0] = sent[:cap]
        for k in range(1, replicas):
            delta_send[g, k] = sent[k * cap : (k + 1) * cap]
        delta_copies.append(
            [None]
            + [
                remote(
                    delta_send.at[g, k],
                    delta_recv.at[g, k],
                    delta_sems.at[g],
                    k,
                    {"replica": behind(k)},
                )
                for k in range(1, replicas)
            ]
        )

    values_load.wait()
    context_copies = []
    for g in range(groups):
        for k in range(1, replicas):
            delta_copies[g][k].wait()
        deltas = mm(unplacing, delta_recv[g].reshape(slots, -1))
        for h in range(heads):
            delta_heads[pl.ds(h, n_rows, stride=heads), :] = deltas[
                :, h * HEAD_DIM : (h + 1) * HEAD_DIM
            ]
        column = g * HEAD_DIM
        new_key = (
            key_value_ref[:, column : column + HEAD_DIM].astype(F32)
            + adapter_scale * deltas[:, group_width : group_width + HEAD_DIM]
        ).astype(BF16)
        new_value = (
            key_value_ref[:, kv_width + column : kv_width + column + HEAD_DIM].astype(F32)
            + adapter_scale * deltas[:, group_width + HEAD_DIM :]
        ).astype(BF16)

        def attend_step(step, carry, g=g, new_key=new_key, new_value=new_value):
            here = heads_of(step)
            plain = base_heads[g, here, :].astype(BF16)
            correction = delta_heads[here, :].astype(BF16)
            scores = base_scores[g, here, :] + (adapter_scale * inverse_root) * score(
                correction, block_of(keys, step, g)
            )
            own_scores = (
                mm(plain, new_key, NT) + adapter_scale * mm(correction, new_key, NT)
            ) * inverse_root
            own_scores = jnp.where(row_hits(step), own_scores, masked_score)
            peak = jnp.maximum(
                jnp.max(scores, axis=1, keepdims=True), jnp.max(own_scores, axis=1, keepdims=True)
            )
            cache_exp = jnp.exp(scores - peak)
            own_exp = jnp.exp(own_scores - peak)
            total = jnp.sum(cache_exp, axis=1, keepdims=True) + jnp.sum(
                own_exp, axis=1, keepdims=True
            )
            share = 1.0 / total
            weights = (cache_exp * share).astype(BF16)
            own_weights = (own_exp * share).astype(BF16)
            found = lax.dot_general(
                weights.reshape(step_blocks, block_heads, block_columns),
                block_of(values, step, g),
                (((2,), (1,)), ((0,), (0,))),
                preferred_element_type=F32,
            ).reshape(step_heads, HEAD_DIM)
            context_heads[here, :] = found + mm(own_weights, new_value)
            return carry

        lax.fori_loop(0, steps, attend_step, 0)
        for h in range(heads):
            column = (g * heads + h) * HEAD_DIM
            context_ref[:, column : column + HEAD_DIM] = context_heads[
                pl.ds(h, n_rows, stride=heads), :
            ].astype(BF16)
        packed = mm(placing, context_ref[:, g * group_width : (g + 1) * group_width]).astype(BF16)
        context_recv[g, 0] = packed[:cap]
        for k in range(1, replicas):
            context_send[g, k] = packed[k * cap : (k + 1) * cap]
        context_copies.append(
            [None]
            + [
                remote(
                    context_send.at[g, k],
                    context_recv.at[g, k],
                    context_sems.at[g],
                    k,
                    {"replica": ahead(k)},
                )
                for k in range(1, replicas)
            ]
        )

    out_down_load.wait()
    out_terms = [0.0 for _ in bundles]
    for g in range(groups):
        for i, bundle in enumerate(bundles):
            for k in bundle:
                if k:
                    context_copies[g][k].wait()
            received = context_recv[g, bundle[0] : bundle[-1] + 1].reshape(len(bundle) * cap, -1)
            out_terms[i] = out_terms[i] + mm(
                out_down[:, g * group_width : (g + 1) * group_width], received, NT
            )
    out_parts = [fold(terms, part) for terms, part in zip(out_terms, selector_parts)]
    out_coeffs = expand(sum_over_tensor(out_parts, out_coeff_recv, out_coeff_sems))
    out_up_load.wait()
    adjust_copies = []
    for g in range(groups):
        sent = (
            adapter_scale * mm(out_coeffs, out_up[:, g * group_width : (g + 1) * group_width])
        ).astype(BF16)
        adjust_recv[g, 0] = sent[:cap]
        for k in range(1, replicas):
            adjust_send[g, k] = sent[k * cap : (k + 1) * cap]
        adjust_copies.append(
            [None]
            + [
                remote(
                    adjust_send.at[g, k],
                    adjust_recv.at[g, k],
                    adjust_sems.at[g],
                    k,
                    {"replica": behind(k)},
                )
                for k in range(1, replicas)
            ]
        )
    for g in range(groups):
        for k in range(1, replicas):
            adjust_copies[g][k].wait()
        adjust_ref[:, g * group_width : (g + 1) * group_width] = mm(
            unplacing, adjust_recv[g].reshape(slots, -1)
        ).astype(BF16)


def local(
    replicas,
    tensors,
    features,
    base_query,
    base_key_value,
    cached_key_rows,
    cached_value_rows,
    cache_length,
    row_adapter_index,
    adapter_storage_slot,
    adapter_down_maps,
    query_up_maps,
    key_value_up_maps,
    output_down_maps,
    output_up_maps,
):
    n_rows, width = features.shape
    own, coeff_width, _ = adapter_down_maps.shape
    rank = coeff_width // 3
    query_width = base_query.shape[1]
    kv_width = base_key_value.shape[2]
    positions = cached_key_rows.shape[1]
    groups = kv_width // HEAD_DIM
    heads = query_width // HEAD_DIM // groups
    group_width = heads * HEAD_DIM
    capacity = min(n_rows // 2, 2 * n_rows // replicas)
    cap = -(-capacity // 16) * 16
    slots = replicas * cap
    score_rows = n_rows * heads

    vmem = pl.BlockSpec(memory_space=pltpu.VMEM)
    anywhere = pl.BlockSpec(memory_space=pl.ANY)

    def pair_sems(*lead):
        return pltpu.SemaphoreType.DMA((*lead, 2, replicas))

    return pl.pallas_call(
        functools.partial(kernel, replicas, tensors, cap, rank),
        out_shape=(
            jax.ShapeDtypeStruct((n_rows, query_width), BF16),
            jax.ShapeDtypeStruct((n_rows, query_width), BF16),
        ),
        in_specs=[vmem] * 6 + [anywhere] * 7,
        out_specs=(vmem, vmem),
        scratch_shapes=[
            pltpu.VMEM(cached_key_rows.shape, BF16),
            pltpu.VMEM(cached_value_rows.shape, BF16),
            pltpu.VMEM((own * coeff_width, width), BF16),
            pltpu.VMEM((own * rank, query_width), BF16),
            pltpu.VMEM((own * rank, 2 * kv_width), BF16),
            pltpu.VMEM((own * rank, query_width), BF16),
            pltpu.VMEM((own * rank, query_width), BF16),
            pltpu.VMEM((replicas, cap, width + LANES), BF16),
            pltpu.VMEM((replicas, cap, width + LANES), BF16),
            pltpu.VMEM((tensors, coeff_width, slots), F32),
            pltpu.VMEM((groups, replicas, cap, group_width + 2 * HEAD_DIM), BF16),
            pltpu.VMEM((groups, replicas, cap, group_width + 2 * HEAD_DIM), BF16),
            pltpu.VMEM((groups, replicas, cap, group_width), BF16),
            pltpu.VMEM((groups, replicas, cap, group_width), BF16),
            pltpu.VMEM((tensors, rank, slots), F32),
            pltpu.VMEM((groups, replicas, cap, group_width), BF16),
            pltpu.VMEM((groups, replicas, cap, group_width), BF16),
            pltpu.VMEM((groups, score_rows, HEAD_DIM), F32),
            pltpu.VMEM((score_rows, HEAD_DIM), F32),
            pltpu.VMEM((score_rows, HEAD_DIM), F32),
            pltpu.VMEM((groups, score_rows, BLOCK_ROWS * positions), F32),
            pltpu.SemaphoreType.DMA((7,)),
            pair_sems(),
            pltpu.SemaphoreType.DMA((2, tensors)),
            pair_sems(groups),
            pair_sems(groups),
            pltpu.SemaphoreType.DMA((2, tensors)),
            pair_sems(groups),
        ],
        compiler_params=pltpu.CompilerParams(
            collective_id=0, has_side_effects=True, vmem_limit_bytes=56 * 1024 * 1024
        ),
    )(
        row_adapter_index.reshape(1, -1),
        adapter_storage_slot.reshape(1, -1),
        cache_length.reshape(1, -1),
        features,
        base_query,
        base_key_value.reshape(n_rows, 2 * kv_width),
        cached_key_rows,
        cached_value_rows,
        adapter_down_maps.reshape(own * coeff_width, width),
        query_up_maps.reshape(own * rank, query_width),
        key_value_up_maps.reshape(own * rank, 2 * kv_width),
        output_down_maps.reshape(own * rank, query_width),
        output_up_maps.reshape(own * rank, query_width),
    )


def solution(mesh):
    return jax.shard_map(
        functools.partial(local, mesh.shape["replica"], mesh.shape["tensor"]),
        mesh=mesh,
        in_specs=(
            P(("groups", "replica"), "tensor"),
            P(("groups", "replica"), "tensor"),
            P(("groups", "replica"), None, "tensor"),
            P(("groups", "replica"), None, "tensor"),
            P(("groups", "replica"), None, "tensor"),
            P(("groups", "replica")),
            P(("groups", "replica")),
            P("groups"),
            P("replica", None, "tensor"),
            P("replica", None, "tensor"),
            P("replica", None, None, "tensor"),
            P("replica", None, "tensor"),
            P("replica", None, "tensor"),
        ),
        out_specs=(P(("groups", "replica"), "tensor"), P(("groups", "replica"), "tensor")),
        check_vma=False,
    )
```

time: 159 us -> 82 us (0.52)
  Pallas kernels: 0 us -> 74.6 us
  waiting for transfers between devices: 58.6 us -> 0 us
  blocking collectives: 46.7 us -> 0 us
  matrix products: 21.1 us -> 0 us
  between operations: 14.3 us -> 0.64 us
  other arithmetic: 5.1 us -> 0 us
  starting transfers between devices: 4.23 us -> 0 us
  local copies, waits for them, and re-layouts: 8.2 us -> 6.5 us
    pallas_call x0 -> x1, Pallas kernels: none -> 74.6 us  [local(): pl.pallas_call(functools.partial(kernel, replicas, tensors, cap, rank), o...]
    all_gather x2 -> x0, waiting for transfers between devices: 42.9 us -> none  [route(): lax.all_gather(source, 'replica', axis=0, tiled=True)]
    dot_general x14 -> x0, matrix products: 21.1 us -> none  [the longest x2 4.62 us: pick_coeffs(): lax.dot_general(scratch_buffer, down_flat, (((1,), (1,)), ((), ())), pref...]
    psum x2 -> x0, blocking collectives: 17.4 us -> none  [reduce_coeffs(): return lax.psum(partial_value, 'tensor').astype(jnp.bfloat16)]
    all_to_all x1 -> x0, blocking collectives: 16.8 us -> none  [send_back(): lax.all_to_all(result, 'replica', split_axis=0, concat_axis=0, tiled=True)]
    all_to_all x1 -> x0, waiting for transfers between devices: 14.9 us -> none  [send_back(): lax.all_to_all(result, 'replica', split_axis=0, concat_axis=0, tiled=True)]
    all_gather x1 -> x0, blocking collectives: 12.6 us -> none  [route(): lax.all_gather(row_codes, 'replica', axis=0, tiled=True)]
    all_to_all x1 -> x0, starting transfers between devices: 4.15 us -> none  [send_back(): lax.all_to_all(result, 'replica', split_axis=0, concat_axis=0, tiled=True)]
  transfers between devices with their start and end apart: 3 -> 0, of which waited for: 3 -> 0; matrix products, arithmetic and copies ran while one was open for 4% -> 0% of each run, Pallas kernels for 0% -> 0%
where the time goes in v1:
time: 82 us; the launch traced here: 81.8 us
  Pallas kernels  74.6 us (91%)
  local copies, waits for them, and re-layouts  6.5 us (8%)
    pallas_call x1, Pallas kernels, local(): pl.pallas_call(functools.partial(kernel, replicas, tensors, cap, rank), o...  74.6 us
    unnamed x4, local copies, waits for them, and re-layouts  6.5 us

profile of v1, /device:TPU:0, one launch (start us, length us, event | category | flops | bytes accessed | tf_op | source)
XLA Modules:
  0.0 81.8 jit_solution(15995259137548644196)
XLA Ops:
  0.6 1.5 %copy.15 = bf16[8,8,2,256]{3,1,2,0:T(8,128)(2,1)} copy(bf16[8,8,2,256]{3,2,1,0:T(2,128)(2,1)} %bitcast.19) | data formatting | bytes 131072
  2.1 1.7 %copy.16 = bf16[32,8,2,256]{3,1,2,0:T(8,128)(2,1)} copy(bf16[32,8,2,256]{3,2,1,0:T(2,128)(2,1)} %bitcast.18) | data formatting | bytes 524288
  3.8 74.6 %shard_map.140 = (bf16[64,2048]{1,0:T(8,128)(2,1)}, bf16[64,2048]{1,0:T(8,128)(2,1)}) custom-call(s32[1,64]{1,0:T(1,128)} %bitcast.20, s32[1,64]{1,0:T(1,128)} %bitcast.21, s32[1,64]{1,0:T(1,128)} %bitcast.22, bf16[64,2048]{1,0:T(8,128)(2,1)} %feature_ref.1, bf16[64,2048]{1,0:T(8,128)(2,1)} %query_ref.1, bf16[64,512]{1,0:T(8,128)(2,1)} %bitcast.17, ...), custom_call_target="tpu_custom_call" | custom-call | tf_op jit(solution)/shard_map/pallas_call | solution.py:486
  78.4 1.7 %copy.19 = bf16[64,2048]{1,0:T(8,128)(2,1)} copy(bf16[64,2048]{1,0:T(8,128)(2,1)} %get-tuple-element.4) | data formatting | bytes 524288
  80.1 1.7 %copy.20 = bf16[64,2048]{1,0:T(8,128)(2,1)} copy(bf16[64,2048]{1,0:T(8,128)(2,1)} %get-tuple-element.5) | data formatting | bytes 524288

commit v2 on v1

--- a/solution.py
+++ b/solution.py
@@ -37,6 +37,7 @@
     replicas,
     tensors,
     cap,
+    halves,
     rank,
     index_ref,
     table_ref,
@@ -52,12 +53,14 @@
     out_down_hbm,
     out_up_hbm,
     context_ref,
-    adjust_ref,
+    adjust_recv,
+    unplacing_ref,
     keys,
     values,
     down,
     query_up,
     key_value_up,
+    key_value_split,
     out_down,
     out_up,
     feature_send,
@@ -69,7 +72,6 @@
     context_recv,
     out_coeff_recv,
     adjust_send,
-    adjust_recv,
     base_heads,
     delta_heads,
     context_heads,
@@ -81,16 +83,19 @@
     context_sems,
     out_coeff_sems,
     adjust_sems,
+    keep_sems,
 ):
     n_rows, width = feature_ref.shape
     query_width = query_ref.shape[1]
-    kv_width = key_value_ref.shape[1] // 2
+    kv_width = key_value_ref.shape[2]
     groups = kv_width // HEAD_DIM
     heads = query_width // HEAD_DIM // groups
     group_width = heads * HEAD_DIM
     positions = key_hbm.shape[1]
     adapters = table_ref.shape[1]
     own = out_down_hbm.shape[0] // rank
+    half_cap = cap // halves
+    half_slots = replicas * half_cap
     slots = replicas * cap
     inverse_root = 1.0 / math.sqrt(HEAD_DIM)
     me = lax.axis_index("replica")
@@ -170,26 +175,41 @@
     before = one_hot(iota((n_rows, n_rows), 0) <= iota((n_rows, n_rows), 1))
     counts = mm(one_hot(owner_hits), before)
     row_rank = jnp.sum(jnp.where(owner_hits, counts, 0.0), axis=0, keepdims=True) - 1.0
-    row_target = relative * cap + row_rank.astype(jnp.int32)
+    row_rank = row_rank.astype(jnp.int32)
+    row_half = row_rank // half_cap
+    row_target = row_half * half_slots + relative * half_cap + row_rank - row_half * half_cap
     placing = one_hot(iota((slots, n_rows), 0) == row_target)
     identity = one_hot(iota((n_rows, n_rows), 0) == iota((n_rows, n_rows), 1))
     unplacing = mm(identity, placing, NT).astype(BF16)
+    unplacing_ref[...] = unplacing
     slot_hits = one_hot(iota((LANES, n_rows), 0) == local_slot)
     selectors = mm(placing, slot_hits, NT).astype(BF16)
 
     packed = mm(placing, feature_ref[...]).astype(BF16)
-    feature_recv[0, :, :width] = packed[:cap]
-    feature_recv[0, :, width:] = selectors[:cap]
-    for k in range(1, replicas):
-        feature_send[k, :, :width] = packed[k * cap : (k + 1) * cap]
-        feature_send[k, :, width:] = selectors[k * cap : (k + 1) * cap]
+
+    def slab(array, half, k):
+        at = half * half_slots + k * half_cap
+        return array[at : at + half_cap]
+
+    for half in range(halves):
+        for k in range(replicas):
+            target = feature_send if k else feature_recv
+            target[half, k, :, :width] = slab(packed, half, k)
+            target[half, k, :, width:] = slab(selectors, half, k)
     pl.semaphore_wait(barrier, replicas + tensors - 2)
-    feature_copies = [None] + [
-        remote(
-            feature_send.at[k], feature_recv.at[k], feature_sems, k, {"replica": ahead(k)}
-        )
-        for k in range(1, replicas)
-    ]
+    def send_features(half):
+        return [
+            remote(
+                feature_send.at[half, k],
+                feature_recv.at[half, k],
+                feature_sems.at[half],
+                k,
+                {"replica": ahead(k)},
+            )
+            for k in range(1, replicas)
+        ]
+
+    feature_copies = [send_features(0)]
 
     score_rows = n_rows * heads
     block_columns = BLOCK_ROWS * positions
@@ -249,29 +269,24 @@
 
     lax.fori_loop(0, steps, base_step, 0)
 
-    bundles = [[k] for k in range(replicas)] if replicas <= 4 else [list(range(replicas))]
+    for half in range(1, halves):
+        for copy in feature_copies[half - 1]:
+            copy.wait()
+        feature_copies.append(send_features(half))
+    key_value_up_load.wait()
+    for i in range(2):
+        key_value_split[i] = key_value_up[:, i, :]
+
     down_load.wait()
-    coeff_parts = []
-    selector_parts = []
+    query_up_load.wait()
     chooser = one_hot(iota((own, LANES), 0) == iota((own, LANES), 1))
 
     def fold(terms, selector):
-        stacked = terms.reshape(own, terms.shape[0] // own, terms.shape[1])
+        stacked = terms.reshape(own, terms.shape[0] // own, half_slots)
         return jnp.sum(stacked * selector[:, None, :], axis=0)
 
-    for bundle in bundles:
-        for k in bundle:
-            if k:
-                feature_copies[k].wait()
-        received = feature_recv[bundle[0] : bundle[-1] + 1].reshape(len(bundle) * cap, -1)
-        selector = mm(chooser, received[:, width:], NT)
-        selector_parts.append(selector)
-        coeff_parts.append(fold(mm(down[...], received[:, :width], NT), selector))
-    selector = jnp.concatenate(selector_parts, axis=1)
-
-    def sum_over_tensor(parts, recv, sems):
-        for bundle, part in zip(bundles, parts):
-            recv[0, :, bundle[0] * cap : (bundle[-1] + 1) * cap] = part
+    def sum_over_tensor(part, recv, sems):
+        recv[0] = part
         copies = [
             remote(
                 recv.at[0],
@@ -289,62 +304,104 @@
             total = total + recv[t]
         return total.astype(BF16).astype(F32)
 
-    def expand(coeffs):
+    def expand(coeffs, selector):
         spread = selector[:, None, :] * coeffs[None, :, :]
-        return spread.reshape(own * rank, slots).T.astype(BF16)
-
-    coeffs = sum_over_tensor(coeff_parts, coeff_recv, coeff_sems)
-    query_coeffs = expand(coeffs[:rank])
-    key_coeffs = expand(coeffs[rank : 2 * rank])
-    value_coeffs = expand(coeffs[2 * rank :])
-
-    query_up_load.wait()
-    key_value_up_load.wait()
+        return spread.reshape(own * rank, half_slots).T.astype(BF16)
+
+    half_selectors = []
     delta_copies = []
+    for half in range(halves):
+        if half == halves - 1:
+            for copy in feature_copies[half]:
+                copy.wait()
+        received = feature_recv[half].reshape(half_slots, -1)
+        selector = mm(chooser, received[:, width:], NT)
+        half_selectors.append(selector)
+        part = fold(mm(down[...], received[:, :width], NT), selector)
+        coeffs = sum_over_tensor(part, coeff_recv.at[half], coeff_sems.at[half])
+        query_coeffs = expand(coeffs[:rank], selector)
+        key_coeffs = expand(coeffs[rank : 2 * rank], selector)
+        value_coeffs = expand(coeffs[2 * rank :], selector)
+        last = half == halves - 1
+        for g in range(groups):
+            head_columns = slice(g * HEAD_DIM, (g + 1) * HEAD_DIM)
+            sent = [
+                mm(query_coeffs, query_up[:, g * group_width : (g + 1) * group_width]),
+                mm(key_coeffs, key_value_split[0, :, head_columns]),
+                mm(value_coeffs, key_value_split[1, :, head_columns]),
+            ]
+            sent = jnp.concatenate([x.astype(BF16) for x in sent], axis=1)
+            for k in range(replicas):
+                target = delta_send if k else delta_recv
+                target[half, k, g] = sent[k * half_cap : (k + 1) * half_cap]
+            if last:
+                delta_copies.append(
+                    [
+                        remote(
+                            delta_send.at[half, k, g],
+                            delta_recv.at[half, k, g],
+                            delta_sems.at[g],
+                            k,
+                            {"replica": behind(k)},
+                        )
+                        for k in reversed(range(1, replicas))
+                    ]
+                )
+        if not last:
+            delta_copies.append(
+                [
+                    remote(
+                        delta_send.at[half, k],
+                        delta_recv.at[half, k],
+                        delta_sems.at[groups + half],
+                        k,
+                        {"replica": behind(k)},
+                    )
+                    for k in reversed(range(1, replicas))
+                ]
+            )
+
+    values_load.wait()
+    for copies in delta_copies[: halves - 1]:
+        for copy in copies:
+            copy.wait()
+    context_copies = [[] for _ in range(halves)]
+
+    def send_context(g, parts):
+        for part in parts:
+            sem = context_sems.at[g if part is None else groups - 1 + part]
+            for k in range(1, replicas):
+                index = (g, k) if part is None else (g, k, part)
+                context_copies[0 if part is None else part].append(
+                    remote(
+                        context_send.at[index],
+                        context_recv.at[index],
+                        sem,
+                        k,
+                        {"replica": ahead(k)},
+                    )
+                )
+
     for g in range(groups):
-        sent = [
-            mm(query_coeffs, query_up[:, g * group_width : (g + 1) * group_width]),
-            mm(key_coeffs, key_value_up[:, g * HEAD_DIM : (g + 1) * HEAD_DIM]),
-            mm(
-                value_coeffs,
-                key_value_up[:, kv_width + g * HEAD_DIM : kv_width + (g + 1) * HEAD_DIM],
-            ),
-        ]
-        sent = jnp.concatenate([x.astype(BF16) for x in sent], axis=1)
-        delta_recv[g, 0] = sent[:cap]
-        for k in range(1, replicas):
-            delta_send[g, k] = sent[k * cap : (k + 1) * cap]
-        delta_copies.append(
-            [None]
-            + [
-                remote(
-                    delta_send.at[g, k],
-                    delta_recv.at[g, k],
-                    delta_sems.at[g],
-                    k,
-                    {"replica": behind(k)},
-                )
-                for k in range(1, replicas)
-            ]
-        )
-
-    values_load.wait()
-    context_copies = []
-    for g in range(groups):
-        for k in range(1, replicas):
-            delta_copies[g][k].wait()
-        deltas = mm(unplacing, delta_recv[g].reshape(slots, -1))
+        for copy in delta_copies[halves - 1 + g]:
+            copy.wait()
+        deltas = 0.0
+        for half in range(halves):
+            deltas = deltas + mm(
+                unplacing[:, half * half_slots : (half + 1) * half_slots],
+                delta_recv[half, :, g].reshape(half_slots, -1),
+            )
         for h in range(heads):
             delta_heads[pl.ds(h, n_rows, stride=heads), :] = deltas[
                 :, h * HEAD_DIM : (h + 1) * HEAD_DIM
             ]
         column = g * HEAD_DIM
         new_key = (
-            key_value_ref[:, column : column + HEAD_DIM].astype(F32)
+            key_value_ref[:, 0, column : column + HEAD_DIM].astype(F32)
             + adapter_scale * deltas[:, group_width : group_width + HEAD_DIM]
         ).astype(BF16)
         new_value = (
-            key_value_ref[:, kv_width + column : kv_width + column + HEAD_DIM].astype(F32)
+            key_value_ref[:, 1, column : column + HEAD_DIM].astype(F32)
             + adapter_scale * deltas[:, group_width + HEAD_DIM :]
         ).astype(BF16)
 
@@ -386,64 +443,60 @@
                 pl.ds(h, n_rows, stride=heads), :
             ].astype(BF16)
         packed = mm(placing, context_ref[:, g * group_width : (g + 1) * group_width]).astype(BF16)
-        context_recv[g, 0] = packed[:cap]
-        for k in range(1, replicas):
-            context_send[g, k] = packed[k * cap : (k + 1) * cap]
-        context_copies.append(
-            [None]
-            + [
-                remote(
-                    context_send.at[g, k],
-                    context_recv.at[g, k],
-                    context_sems.at[g],
-                    k,
-                    {"replica": ahead(k)},
-                )
-                for k in range(1, replicas)
-            ]
-        )
+        for half in range(halves):
+            for k in range(replicas):
+                target = context_send if k else context_recv
+                target[g, k, half] = slab(packed, half, k)
+        if g < groups - 1:
+            send_context(g, [None])
+    send_context(groups - 1, [0])
 
     out_down_load.wait()
-    out_terms = [0.0 for _ in bundles]
-    for g in range(groups):
-        for i, bundle in enumerate(bundles):
-            for k in bundle:
-                if k:
-                    context_copies[g][k].wait()
-            received = context_recv[g, bundle[0] : bundle[-1] + 1].reshape(len(bundle) * cap, -1)
-            out_terms[i] = out_terms[i] + mm(
-                out_down[:, g * group_width : (g + 1) * group_width], received, NT
-            )
-    out_parts = [fold(terms, part) for terms, part in zip(out_terms, selector_parts)]
-    out_coeffs = expand(sum_over_tensor(out_parts, out_coeff_recv, out_coeff_sems))
     out_up_load.wait()
     adjust_copies = []
-    for g in range(groups):
-        sent = (
-            adapter_scale * mm(out_coeffs, out_up[:, g * group_width : (g + 1) * group_width])
-        ).astype(BF16)
-        adjust_recv[g, 0] = sent[:cap]
-        for k in range(1, replicas):
-            adjust_send[g, k] = sent[k * cap : (k + 1) * cap]
-        adjust_copies.append(
-            [None]
-            + [
-                remote(
-                    adjust_send.at[g, k],
-                    adjust_recv.at[g, k],
-                    adjust_sems.at[g],
-                    k,
-                    {"replica": behind(k)},
-                )
-                for k in range(1, replicas)
-            ]
+    for half in range(halves):
+        for copy in context_copies[half]:
+            copy.wait()
+        if half < halves - 1:
+            send_context(groups - 1, [half + 1])
+        terms = 0.0
+        for g in range(groups):
+            terms = terms + mm(
+                out_down[:, g * group_width : (g + 1) * group_width],
+                context_recv[g, :, half].reshape(half_slots, group_width),
+                NT,
+            )
+        selector = half_selectors[half]
+        coeffs = sum_over_tensor(
+            fold(terms, selector), out_coeff_recv.at[half], out_coeff_sems.at[half]
         )
-    for g in range(groups):
-        for k in range(1, replicas):
-            adjust_copies[g][k].wait()
-        adjust_ref[:, g * group_width : (g + 1) * group_width] = mm(
-            unplacing, adjust_recv[g].reshape(slots, -1)
-        ).astype(BF16)
+        sent = (adapter_scale * mm(expand(coeffs, selector), out_up[...])).astype(BF16)
+        for k in range(replicas):
+            adjust_send[half, k] = sent[k * half_cap : (k + 1) * half_cap]
+        kept = pltpu.make_async_copy(
+            adjust_send.at[half, 0], adjust_recv.at[half, 0], keep_sems.at[half]
+        )
+        kept.start()
+        adjust_copies.append(kept)
+        adjust_copies += [
+            remote(
+                adjust_send.at[half, k],
+                adjust_recv.at[half, k],
+                adjust_sems.at[half],
+                k,
+                {"replica": behind(k)},
+            )
+            for k in reversed(range(1, replicas))
+        ]
+    for copy in adjust_copies:
+        copy.wait()
+
+
+def finish(context_ref, received_ref, unplacing_ref, context_out, adjust_ref):
+    context_out[...] = context_ref[...]
+    adjust_ref[...] = mm(
+        unplacing_ref[...], received_ref[...].reshape(-1, adjust_ref.shape[1])
+    ).astype(BF16)
 
 
 def local(
@@ -472,8 +525,12 @@
     groups = kv_width // HEAD_DIM
     heads = query_width // HEAD_DIM // groups
     group_width = heads * HEAD_DIM
+    delta_width = group_width + 2 * HEAD_DIM
     capacity = min(n_rows // 2, 2 * n_rows // replicas)
     cap = -(-capacity // 16) * 16
+    halves = 2 if cap % 32 == 0 else 1
+    half_cap = cap // halves
+    half_slots = replicas * half_cap
     slots = replicas * cap
     score_rows = n_rows * heads
 
@@ -483,43 +540,45 @@
     def pair_sems(*lead):
         return pltpu.SemaphoreType.DMA((*lead, 2, replicas))
 
-    return pl.pallas_call(
-        functools.partial(kernel, replicas, tensors, cap, rank),
+    context, received, unplacing = pl.pallas_call(
+        functools.partial(kernel, replicas, tensors, cap, halves, rank),
         out_shape=(
             jax.ShapeDtypeStruct((n_rows, query_width), BF16),
-            jax.ShapeDtypeStruct((n_rows, query_width), BF16),
+            jax.ShapeDtypeStruct((halves, replicas, half_cap, query_width), BF16),
+            jax.ShapeDtypeStruct((n_rows, slots), BF16),
         ),
         in_specs=[vmem] * 6 + [anywhere] * 7,
-        out_specs=(vmem, vmem),
+        out_specs=(vmem, anywhere, vmem),
         scratch_shapes=[
             pltpu.VMEM(cached_key_rows.shape, BF16),
             pltpu.VMEM(cached_value_rows.shape, BF16),
             pltpu.VMEM((own * coeff_width, width), BF16),
             pltpu.VMEM((own * rank, query_width), BF16),
-            pltpu.VMEM((own * rank, 2 * kv_width), BF16),
+            pltpu.VMEM((own * rank, 2, kv_width), BF16),
+            pltpu.VMEM((2, own * rank, kv_width), BF16),
             pltpu.VMEM((own * rank, query_width), BF16),
             pltpu.VMEM((own * rank, query_width), BF16),
-            pltpu.VMEM((replicas, cap, width + LANES), BF16),
-            pltpu.VMEM((replicas, cap, width + LANES), BF16),
-            pltpu.VMEM((tensors, coeff_width, slots), F32),
-            pltpu.VMEM((groups, replicas, cap, group_width + 2 * HEAD_DIM), BF16),
-            pltpu.VMEM((groups, replicas, cap, group_width + 2 * HEAD_DIM), BF16),
-            pltpu.VMEM((groups, replicas, cap, group_width), BF16),
-            pltpu.VMEM((groups, replicas, cap, group_width), BF16),
-            pltpu.VMEM((tensors, rank, slots), F32),
-            pltpu.VMEM((groups, replicas, cap, group_width), BF16),
-            pltpu.VMEM((groups, replicas, cap, group_width), BF16),
+            pltpu.VMEM((halves, replicas, half_cap, width + LANES), BF16),
+            pltpu.VMEM((halves, replicas, half_cap, width + LANES), BF16),
+            pltpu.VMEM((halves, tensors, coeff_width, half_slots), F32),
+            pltpu.VMEM((halves, replicas, groups, half_cap, delta_width), BF16),
+            pltpu.VMEM((halves, replicas, groups, half_cap, delta_width), BF16),
+            pltpu.VMEM((groups, replicas, halves, half_cap, group_width), BF16),
+            pltpu.VMEM((groups, replicas, halves, half_cap, group_width), BF16),
+            pltpu.VMEM((halves, tensors, rank, half_slots), F32),
+            pltpu.VMEM((halves, replicas, half_cap, query_width), BF16),
             pltpu.VMEM((groups, score_rows, HEAD_DIM), F32),
             pltpu.VMEM((score_rows, HEAD_DIM), F32),
             pltpu.VMEM((score_rows, HEAD_DIM), F32),
             pltpu.VMEM((groups, score_rows, BLOCK_ROWS * positions), F32),
             pltpu.SemaphoreType.DMA((7,)),
-            pair_sems(),
-            pltpu.SemaphoreType.DMA((2, tensors)),
-            pair_sems(groups),
-            pair_sems(groups),
-            pltpu.SemaphoreType.DMA((2, tensors)),
-            pair_sems(groups),
+            pair_sems(halves),
+            pltpu.SemaphoreType.DMA((halves, 2, tensors)),
+            pair_sems(groups + halves - 1),
+            pair_sems(groups + halves - 1),
+            pltpu.SemaphoreType.DMA((halves, 2, tensors)),
+            pair_sems(halves),
+            pltpu.SemaphoreType.DMA((halves,)),
         ],
         compiler_params=pltpu.CompilerParams(
             collective_id=0, has_side_effects=True, vmem_limit_bytes=56 * 1024 * 1024
@@ -530,15 +589,25 @@
         cache_length.reshape(1, -1),
         features,
         base_query,
-        base_key_value.reshape(n_rows, 2 * kv_width),
+        base_key_value,
         cached_key_rows,
         cached_value_rows,
         adapter_down_maps.reshape(own * coeff_width, width),
         query_up_maps.reshape(own * rank, query_width),
-        key_value_up_maps.reshape(own * rank, 2 * kv_width),
+        key_value_up_maps.reshape(own * rank, 2, kv_width),
         output_down_maps.reshape(own * rank, query_width),
         output_up_maps.reshape(own * rank, query_width),
     )
+    return pl.pallas_call(
+        finish,
+        out_shape=(
+            jax.ShapeDtypeStruct((n_rows, query_width), BF16),
+            jax.ShapeDtypeStruct((n_rows, query_width), BF16),
+        ),
+        in_specs=[vmem] * 3,
+        out_specs=(vmem, vmem),
+        compiler_params=pltpu.CompilerParams(vmem_limit_bytes=56 * 1024 * 1024),
+    )(context, received, unplacing)
 
 
 def solution(mesh):

time: 82 us -> 65.1 us (0.79)
  Pallas kernels: 74.6 us -> 64.3 us
  local copies, waits for them, and re-layouts: 6.5 us -> 0 us
    pallas_call x1 -> x2, Pallas kernels: 74.6 us -> 64.3 us  [the longest x1 62.3 us: local(): pl.pallas_call(functools.partial(kernel, replicas, tensors, cap, halves,...]
    unnamed x4 -> x0, local copies, waits for them, and re-layouts: 6.5 us -> none
where the time goes in v2:
time: 65.1 us; the launch traced here: 65 us
  Pallas kernels  64.3 us (99%)
    pallas_call x1, Pallas kernels, local(): pl.pallas_call(functools.partial(kernel, replicas, tensors, cap, halves,...  62.3 us
    pallas_call x1, Pallas kernels, local(): pl.pallas_call(finish, out_shape=(jax.ShapeDtypeStruct((n_rows, query_wid...  2.04 us

profile of v2, /device:TPU:0, one launch (start us, length us, event | category | flops | bytes accessed | tf_op | source)
XLA Modules:
  0.0 65.0 jit_solution(16718433164974890399)
XLA Ops:
  0.6 62.3 %shard_map.140 = (bf16[64,2048]{1,0:T(8,128)(2,1)}, bf16[2,4,16,2048]{3,2,1,0:T(8,128)(2,1)}, bf16[64,128]{1,0:T(8,128)(2,1)}) custom-call(s32[1,64]{1,0:T(1,128)} %bitcast.13, s32[1,64]{1,0:T(1,128)} %bitcast.14, s32[1,64]{1,0:T(1,128)} %bitcast.15, bf16[64,2048]{1,0:T(8,128)(2,1)} %feature_ref.1, bf16[64,2048]{1,0:T(8,128)(2,1)} %query_ref.1, ...), custom_call_target="tpu_custom_call" | custom-call | tf_op jit(solution)/shard_map/pallas_call | solution.py:543
  62.9 2.0 %shard_map.141 = (bf16[64,2048]{1,0:T(8,128)(2,1)}, bf16[64,2048]{1,0:T(8,128)(2,1)}) custom-call(bf16[64,2048]{1,0:T(8,128)(2,1)} %get-tuple-element.5.context_ref, bf16[2,4,16,2048]{3,2,1,0:T(8,128)(2,1)} %get-tuple-element.6.received_ref, bf16[64,128]{1,0:T(8,128)(2,1)} %get-tuple-element.7.unplacing_ref), custom_call_target="tpu_custom_call" | custom-call | tf_op jit(solution)/shard_map/pallas_call | solution.py:601

commit v3 on v2

--- a/solution.py
+++ b/solution.py
@@ -179,29 +179,37 @@
     row_half = row_rank // half_cap
     row_target = row_half * half_slots + relative * half_cap + row_rank - row_half * half_cap
     placing = one_hot(iota((slots, n_rows), 0) == row_target)
-    identity = one_hot(iota((n_rows, n_rows), 0) == iota((n_rows, n_rows), 1))
-    unplacing = mm(identity, placing, NT).astype(BF16)
-    unplacing_ref[...] = unplacing
-    slot_hits = one_hot(iota((LANES, n_rows), 0) == local_slot)
-    selectors = mm(placing, slot_hits, NT).astype(BF16)
-
-    packed = mm(placing, feature_ref[...]).astype(BF16)
+    slot_hits = [
+        one_hot(iota((LANES, n_rows), 0) == local_slot + half * own) for half in range(halves)
+    ]
+
 
     def slab(array, half, k):
         at = half * half_slots + k * half_cap
         return array[at : at + half_cap]
 
-    for half in range(halves):
+    def pack_features(half):
+        chosen = placing[half * half_slots : (half + 1) * half_slots]
+        packed = mm(chosen, feature_ref[...]).astype(BF16)
         for k in range(replicas):
             target = feature_send if k else feature_recv
-            target[half, k, :, :width] = slab(packed, half, k)
-            target[half, k, :, width:] = slab(selectors, half, k)
+            target[half, k, :, :width] = packed[k * half_cap : (k + 1) * half_cap]
+
+    selectors = 0.0
+    for half in range(halves):
+        chosen = placing[half * half_slots : (half + 1) * half_slots]
+        selectors = selectors + mm(chosen, slot_hits[half], NT)
+    selectors = selectors.astype(BF16)
+    for k in range(replicas):
+        target = feature_send if k else feature_recv
+        target[0, k, :, width:] = selectors[k * half_cap : (k + 1) * half_cap]
+    pack_features(0)
     pl.semaphore_wait(barrier, replicas + tensors - 2)
     def send_features(half):
         return [
             remote(
-                feature_send.at[half, k],
-                feature_recv.at[half, k],
+                feature_send.at[half, k, :, pl.ds(0, width if half else width + LANES)],
+                feature_recv.at[half, k, :, pl.ds(0, width if half else width + LANES)],
                 feature_sems.at[half],
                 k,
                 {"replica": ahead(k)},
@@ -210,6 +218,11 @@
         ]
 
     feature_copies = [send_features(0)]
+    for half in range(1, halves):
+        pack_features(half)
+    identity = one_hot(iota((n_rows, n_rows), 0) == iota((n_rows, n_rows), 1))
+    unplacing = mm(identity, placing, NT).astype(BF16)
+    unplacing_ref[...] = unplacing
 
     score_rows = n_rows * heads
     block_columns = BLOCK_ROWS * positions
@@ -269,17 +282,16 @@
 
     lax.fori_loop(0, steps, base_step, 0)
 
+    key_value_up_load.wait()
+    for i in range(2):
+        key_value_split[i] = key_value_up[:, i, :]
+
     for half in range(1, halves):
         for copy in feature_copies[half - 1]:
             copy.wait()
         feature_copies.append(send_features(half))
-    key_value_up_load.wait()
-    for i in range(2):
-        key_value_split[i] = key_value_up[:, i, :]
-
     down_load.wait()
     query_up_load.wait()
-    chooser = one_hot(iota((own, LANES), 0) == iota((own, LANES), 1))
 
     def fold(terms, selector):
         stacked = terms.reshape(own, terms.shape[0] // own, half_slots)
@@ -315,7 +327,8 @@
             for copy in feature_copies[half]:
                 copy.wait()
         received = feature_recv[half].reshape(half_slots, -1)
-        selector = mm(chooser, received[:, width:], NT)
+        chooser = one_hot(iota((own, LANES), 0) + half * own == iota((own, LANES), 1))
+        selector = mm(chooser, feature_recv[0].reshape(half_slots, -1)[:, width:], NT)
         half_selectors.append(selector)
         part = fold(mm(down[...], received[:, :width], NT), selector)
         coeffs = sum_over_tensor(part, coeff_recv.at[half], coeff_sems.at[half])

time: 65.1 us -> 64.6 us (level)
  no operation moved by 1% of the time
where the time goes in v3:
time: 64.6 us; the launch traced here: 64.5 us
  Pallas kernels  63.8 us (99%)
    pallas_call x1, Pallas kernels, local(): pl.pallas_call(functools.partial(kernel, replicas, tensors, cap, halves,...  61.8 us
    pallas_call x1, Pallas kernels, local(): pl.pallas_call(finish, out_shape=(jax.ShapeDtypeStruct((n_rows, query_wid...  2.04 us

profile of v3, /device:TPU:0, one launch (start us, length us, event | category | flops | bytes accessed | tf_op | source)
XLA Modules:
  0.0 64.5 jit_solution(6230286577415437518)
XLA Ops:
  0.6 61.8 %shard_map.140 = (bf16[64,2048]{1,0:T(8,128)(2,1)}, bf16[2,4,16,2048]{3,2,1,0:T(8,128)(2,1)}, bf16[64,128]{1,0:T(8,128)(2,1)}) custom-call(s32[1,64]{1,0:T(1,128)} %bitcast.13, s32[1,64]{1,0:T(1,128)} %bitcast.14, s32[1,64]{1,0:T(1,128)} %bitcast.15, bf16[64,2048]{1,0:T(8,128)(2,1)} %feature_ref.1, bf16[64,2048]{1,0:T(8,128)(2,1)} %query_ref.1, ...), custom_call_target="tpu_custom_call" | custom-call | tf_op jit(solution)/shard_map/pallas_call | solution.py:556
  62.4 2.0 %shard_map.141 = (bf16[64,2048]{1,0:T(8,128)(2,1)}, bf16[64,2048]{1,0:T(8,128)(2,1)}) custom-call(bf16[64,2048]{1,0:T(8,128)(2,1)} %get-tuple-element.5.context_ref, bf16[2,4,16,2048]{3,2,1,0:T(8,128)(2,1)} %get-tuple-element.6.received_ref, bf16[64,128]{1,0:T(8,128)(2,1)} %get-tuple-element.7.unplacing_ref), custom_call_target="tpu_custom_call" | custom-call | tf_op jit(solution)/shard_map/pallas_call | solution.py:614
